TPU v7x, 1024 devices: a whole 8x8x8 slice. The times are simulated.
1024 devices in a mesh: dp: 8 (over x_hi, core), tensor: 16 (over z, x_lo), expert: 8 (over y).
Axes of the slice: x: 8 (x_hi: 4, x_lo: 2; x = x_hi * 2 + x_lo), y: 8, z: 8, core: 2. Of those that a mesh axis runs over, the one named last changes fastest.
Arguments:
- tokens: bfloat16 [8192, 3072], P(('dp', 'expert'), 'tensor'), may hold values from -6 to 6
- expert_ids: int32 [8192, 4], P(('dp', 'expert')), may hold values from 0 to 7, all different within a row; in each aligned block of 128 rows (0 to 127, 128 to 255, ...) at most 72 rows name the same one
- gate_raw: float32 [8192, 4], P(('dp', 'expert')), may hold values from 0.05 to 10, as said below
- w_gate: bfloat16 [8, 3072, 5376], P('expert', None, 'tensor'), may hold values from -0.109375 to 0.109375
- w_up: bfloat16 [8, 3072, 5376], P('expert', None, 'tensor'), may hold values from -0.109375 to 0.109375
- w_down: bfloat16 [8, 5376, 3072], P('expert', 'tensor'), may hold values from -0.078125 to 0.078125
Outputs:
- mixed: bfloat16 [8192, 3072], P(('dp', 'expert'), 'tensor')
- balance: float32 [], replicated
Inputs may be any that keep to these rules, and one draw needn't show every extreme that they name: `expert_ids`: each row names 4 different experts; within each aligned block of 128 rows (the rows of one device) no expert is named by more than 72 rows, a bound that some block reaches. `gate_raw`: Positive.
All inputs are finite; a program needn't handle non-finite values.
Results may differ from a plain program's by a relative error of at most 0.024.
Values may be sent and summed in bfloat16 or wider, within the bound.
A program may use at most 64 MiB of HBM per device.

v0:
```python
import jax
import jax.numpy as jnp
from jax import lax
from jax.sharding import PartitionSpec as P


def body(tokens, expert_ids, gate_raw, w_gate, w_up, w_down):
    tok_rows, local_feat = tokens.shape
    top_count = expert_ids.shape[1]
    experts = lax.axis_size("expert")
    capacity = tok_rows * top_count * 9 // (8 * experts)
    slot_total = experts * capacity
    gate_norm = gate_raw / jnp.sum(gate_raw, axis=1, keepdims=True)
    flat_ids = expert_ids.reshape(-1)
    flat_raw = gate_raw.reshape(-1)
    expert_range = jnp.arange(experts, dtype=jnp.int32)
    one_hot = (flat_ids[:, None] == expert_range[None, :]).astype(jnp.int32)
    running = jnp.cumsum(one_hot, axis=0) - 1
    slot_index = jnp.sum(running * one_hot, axis=1)
    slot_target = flat_ids * capacity + slot_index
    source_rows = jnp.arange(flat_ids.shape[0], dtype=jnp.int32) // top_count
    gate_mass = jnp.sum(one_hot.astype(jnp.float32) * flat_raw[:, None], axis=0)
    mass_all = lax.psum(gate_mass, ("dp", "expert"))
    total_tokens = tok_rows * lax.axis_size("dp") * experts
    balance = experts * jnp.sum((mass_all / total_tokens) ** 2)
    send_rows = (
        jnp.zeros((slot_total, local_feat), jnp.bfloat16).at[slot_target].set(tokens[source_rows])
    )
    received = lax.all_to_all(
        send_rows.reshape(experts, capacity, local_feat),
        "expert",
        split_axis=0,
        concat_axis=0,
        tiled=True,
    )
    gate_matrix = w_gate[0]
    up_matrix = w_up[0]
    down_matrix = w_down[0]
    piece = lax.all_gather(received, "tensor", axis=2, tiled=True)
    flat_rows = piece.reshape(-1, piece.shape[2])
    gate_sum = jnp.dot(flat_rows, gate_matrix, preferred_element_type=jnp.float32)
    up_sum = jnp.dot(flat_rows, up_matrix, preferred_element_type=jnp.float32)
    hidden = (jax.nn.silu(gate_sum) * up_sum).astype(jnp.bfloat16)
    summed = lax.psum_scatter(
        lax.dot_general(
            down_matrix, hidden, (((0,), (1,)), ((), ())), preferred_element_type=jnp.float32
        ).astype(jnp.bfloat16),
        "tensor",
        scatter_dimension=0,
        tiled=True,
    )
    results = summed.reshape(local_feat, experts, capacity)
    returned_rows = lax.all_to_all(
        results, "expert", split_axis=1, concat_axis=1, tiled=True
    ).reshape(local_feat, slot_total)
    picked = returned_rows[:, slot_target].astype(jnp.float32)
    weighted = picked.reshape(local_feat, tok_rows, top_count) * gate_norm[None, :, :]
    mixed_cols = jnp.sum(weighted, axis=2)
    mixed = jnp.transpose(mixed_cols).astype(jnp.bfloat16)
    return (mixed, balance)


def solution(mesh):
    return jax.shard_map(
        body,
        mesh=mesh,
        in_specs=(
            P(("dp", "expert"), "tensor"),
            P(("dp", "expert"), None),
            P(("dp", "expert"), None),
            P("expert", None, "tensor"),
            P("expert", None, "tensor"),
            P("expert", "tensor", None),
        ),
        out_specs=(P(("dp", "expert"), "tensor"), P()),
        check_vma=False,
    )
```

profile of v0, /device:TPU:16, one launch (start us, length us, event | category | flops | bytes accessed | tf_op | source)
XLA Modules:
  0.0 393.0 jit_solution(14019427816446593720)
XLA Ops:
  7.2 0.9 copy.24
  8.2 0.1 eq.29
  8.3 0.1 eq.25
  8.4 0.7 broadcast_multiply_fusion
  9.1 1.1 reduce-window.6
  10.2 0.2 slice_reduce_fusion
  10.5 0.1 copy.23
  10.6 0.1 mul.46
  10.7 0.9 copy.26
  11.6 0.1 fusion.18
  11.7 3.8 scatter_custom_fusion
  15.6 24.7 %all_to_all.10 = bf16[8,72,192]{2,1,0:T(8,128)(2,1)S(1)} all-to-all(bf16[8,72,192]{2,1,0:T(8,128)(2,1)S(1)} %bitcast.43), channel_id=1, replica_groups=mesh['dp'=8,'tensor'=16,'expert'=8] {'expert'}, dimensions={0} | all-to-all | bytes 442368 | tf_op jit(solution)/shard_map/all_to_all | solution.py:29
  40.3 1.0 copy.27
  41.4 150.4 %all-gather.2.cloned.1.call-done = bf16[8,72,3072]{1,0,2:T(8,128)(2,1)} async-done(((bf16[8,72,192]{1,0,2:T(8,128)(2,1)}), bf16[8,72,3072]{1,0,2:T(8,128)(2,1)}) %all-gather.2.cloned.1.call-update) | async-done | bytes 3538960 | tf_op jit(solution)/shard_map/all_gather | solution.py:39
  191.7 8.4 %copy.28 = bf16[8,72,3072]{2,1,0:T(8,128)(2,1)} copy(bf16[8,72,3072]{1,0,2:T(8,128)(2,1)} %all-gather.2.cloned.1.call-done) | data formatting | bytes 7077888 | tf_op jit(solution)/shard_map/all_gather | solution.py:39
  200.2 4.4 %fusion.4 = f32[576,336]{0,1:T(8,128)S(1)} fusion(bf16[576,3072]{1,0:T(8,128)(2,1)} %bitcast.41, bf16[1,3072,336]{1,2,0:T(8,128)(2,1)} %param.9), kind=kOutput, calls=%fused_computation.8 | convolution fusion | flops 1189085184 | bytes 6377472 | tf_op jit(solution)/shard_map/dot_general | solution.py:41
  204.6 9.3 %fusion = bf16[3072,576]{0,1:T(8,128)(2,1)} fusion(bf16[1,336,3072]{2,1,0:T(8,128)(2,1)S(1)} %copy-done, bf16[576,3072]{1,0:T(8,128)(2,1)} %bitcast.42, bf16[1,3072,336]{1,2,0:T(8,128)(2,1)} %param.10, f32[576,336]{0,1:T(8,128)S(1)} %fusion.4), kind=kOutput, calls=%fused_computation.4 | convolution fusion | flops 2381101056 | bytes 11980800 | tf_op jit(solution)/shard_map/dot_general | solution.py:45
  213.9 6.1 %copy.32 = bf16[3072,576]{1,0:T(8,128)(2,1)} copy(bf16[3072,576]{0,1:T(8,128)(2,1)} %fusion) | data formatting | bytes 7077888
  220.0 0.7 copy-done.1
  220.7 0.1 copy.30
  220.8 0.1 mul.52
  220.9 0.1 multiply_reduce_fusion.1
  221.0 142.2 %psum.7 = f32[8]{0:T(128)S(1)} all-reduce(f32[8]{0:T(128)S(1)} %multiply_reduce_fusion.1), channel_id=1, replica_groups=mesh['dp'=8,'tensor'=16,'expert'=8] {'dp','expert'}, use_global_device_ids=true, to_apply=%region_8.9 | all-reduce | flops 8 | bytes 64 | tf_op jit(solution)/shard_map/psum | solution.py:23
  363.2 1.8 copy.33
  365.0 7.3 %all-to-all-start.1 = ((bf16[192,8,72]{0,2,1:T(8,128)(2,1)}), bf16[192,8,72]{0,2,1:T(8,128)(2,1)S(1)}, u32[]{:S(2)}, u32[]{:S(2)}) async-start(bf16[192,8,72]{0,2,1:T(8,128)(2,1)} %bitcast.11), calls=%async_computation.1 | async-start | bytes 589824 | tf_op jit(solution)/shard_map/all_to_all | solution.py:53
  372.3 0.1 copy.29
  372.5 0.6 multiply_reduce_fusion.2
  373.7 8.0 %all-to-all-done.1 = bf16[192,8,72]{0,2,1:T(8,128)(2,1)S(1)} async-done(((bf16[192,8,72]{0,2,1:T(8,128)(2,1)}), bf16[192,8,72]{0,2,1:T(8,128)(2,1)S(1)}, u32[]{:S(2)}, u32[]{:S(2)}) %all-to-all-start.1) | async-done | bytes 221216 | tf_op jit(solution)/shard_map/all_to_all | solution.py:53
  381.7 1.9 gather_fusion
  383.7 0.2 reshape.119
  383.9 0.4 multiply_reduce_fusion
  384.3 0.7 copy.31
  (18 shorter events, 0.3 us)
Async XLA Ops:
  7.2 197.4 %copy-start = (bf16[1,336,3072]{2,1,0:T(8,128)(2,1)S(1)}, bf16[1,336,3072]{2,1,0:T(8,128)(2,1)}, u32[]{:S(2)}) copy-start(bf16[1,336,3072]{2,1,0:T(8,128)(2,1)} %param.11) | copy-start | bytes 6193156
  7.2 184.5 %all-gather.2.cloned.1.call-start = ((), (), s32[]{:S(2)}) async-start(), calls=%async_computation.3 | async-start | bytes 6684672 | tf_op jit(solution)/shard_map/all_gather | solution.py:39
  41.3 321.9 %reduce-scatter.4.cloned.1.call-start = ((), (), s32[]{:S(2)}) async-start(), calls=%async_computation.4 | async-start | bytes 4177920
  220.0 0.7 copy-start.1
  365.0 16.7 %all-to-all-start.1 = ((bf16[192,8,72]{0,2,1:T(8,128)(2,1)}), bf16[192,8,72]{0,2,1:T(8,128)(2,1)S(1)}, u32[]{:S(2)}, u32[]{:S(2)}) async-start(bf16[192,8,72]{0,2,1:T(8,128)(2,1)} %bitcast.11), calls=%async_computation.1 | async-start | bytes 589824 | tf_op jit(solution)/shard_map/all_to_all | solution.py:53
Sparse Core Ops, SparseCore 0:
  41.4 150.2 all-gather.1
  220.2 100.1 reduce-scatter.3
where the time goes:
time: 394 us; the launch traced here: 393 us
  blocking collectives  167 us (42%)
  waiting for transfers between devices  158 us (40%)
  local copies, waits for them, and re-layouts  27.5 us (7%)
  between operations  15.9 us (4%)
  matrix products  13.8 us (4%)
  starting transfers between devices  7.38 us (2%)
    all_gather x1, waiting for transfers between devices, body(): piece = lax.all_gather(received, 'tensor', axis=2, tiled=True)  150 us
    psum x1, blocking collectives, body(): mass_all = lax.psum(gate_mass, ('dp', 'expert'))  142 us
    all_to_all x1, blocking collectives, body(): lax.all_to_all(send_rows.reshape(experts, capacity, local_feat), 'expert'...  24.7 us
    unnamed x10, local copies, waits for them, and re-layouts  11.2 us
    dot_general x1, matrix products, body(): lax.dot_general(down_matrix, hidden, (((0,), (1,)), ((), ())), preferred_...  9.31 us
    all_gather x1, local copies, waits for them, and re-layouts, body(): piece = lax.all_gather(received, 'tensor', axis=2, tiled=True)  8.44 us
    all_to_all x1, waiting for transfers between devices, body(): lax.all_to_all(results, 'expert', split_axis=1, concat_axis=1, tiled=True)  8.01 us
  transfers between devices with their start and end apart: 3, of which 2 were waited for; matrix products, arithmetic and copies ran while one was open for 0% of the time, Pallas kernels for 0%

commit v1 on v0

v1 whole, which is shorter than its diff:
```python
import jax
import jax.numpy as jnp
from jax import lax
from jax.experimental import pallas as pl
from jax.experimental.pallas import tpu as pltpu
from jax.sharding import PartitionSpec as P

MESH = pl.DeviceIdType.MESH
F32 = jnp.float32
BF16 = jnp.bfloat16

NZ = 8
NY = 8
CAP = 72
PAD = 80
SRC = 4
HALF = SRC * CAP
ROWS = 2 * HALF
A = 160
BLO, B = A, 256
P1, OWN1 = HALF, HALF - A
P2 = ROWS - A


def remote(src, dst, send, recv, device):
    return pltpu.make_async_remote_copy(
        src_ref=src,
        dst_ref=dst,
        send_sem=send,
        recv_sem=recv,
        device_id=device,
        device_id_type=MESH,
    )


def kernel(
    tok, ids, raw, wg_hbm, wu_hbm, wd_hbm, out, bal,
    wg, wu, wd, tokx, wide, onehot, gates, slots, landing, gath, acc_g, acc_u, hid,
    sa, sb, ra, rb, xs, xr, cross_s, cross_r, back_s, back_r, mix_s, mix_r, mass, bfly,
    w_sem, tok_sem, y_send, y_recv, own_send, own_recv,
    g_send, g_recv, xf_send, xf_recv, r_send, r_recv, xs_send, xs_recv,
    cr_sem, bk_send, bk_recv, mx_sem, ms_send, ms_recv, bf_send, bf_recv,
):
    dp, ten, y = lax.axis_index("dp"), lax.axis_index("tensor"), lax.axis_index("expert")
    tokens, feat = tok.shape
    width = 2 * feat
    z, xl = ten // 2, lax.rem(ten, 2)
    turn = 1 - 2 * lax.rem(dp, 2)
    par = lax.rem(xl + y, 2)
    me_half = y // 2

    def at(steps):
        return lax.rem(z + turn * steps + 2 * NZ, NZ)

    partner = {"tensor": z * 2 + 1 - xl}
    ahead = {"tensor": at(1) * 2 + xl}
    behind = {"tensor": at(-1) * 2 + xl}

    def flip(bit):
        return dp + bit - 2 * bit * lax.rem(dp // bit, 2)

    loads = [
        pltpu.make_async_copy(src.at[0], dst, w_sem.at[i])
        for i, (src, dst) in enumerate(((wg_hbm, wg), (wu_hbm, wu), (wd_hbm, wd)))
    ]
    for load in loads:
        load.start()

    barrier = pltpu.get_barrier_semaphore()
    peers = [{"expert": lax.rem(y + i, NY)} for i in range(1, NY)]
    peers += [partner, ahead, behind] + [{"dp": flip(bit)} for bit in (1, 2, 4)]
    for peer in peers:
        pl.semaphore_signal(barrier, inc=1, device_id=peer, device_id_type=MESH)

    lane = lax.broadcasted_iota(jnp.int32, (tokens, 128), 1)
    ids_v, raw_v = ids[...], raw[...]
    norm_v = raw_v / jnp.sum(raw_v, axis=1, keepdims=True)
    named = jnp.zeros((tokens, 128), F32)
    weight = jnp.zeros((tokens, 128), F32)
    share = jnp.zeros((tokens, 128), F32)
    for k in range(ids.shape[1]):
        hit = ids_v[:, k : k + 1] == lane
        named = jnp.where(hit, 1.0, named)
        weight = jnp.where(hit, raw_v[:, k : k + 1], weight)
        share = jnp.where(hit, norm_v[:, k : k + 1], share)
    row = lax.broadcasted_iota(jnp.int32, (tokens, tokens), 0)
    col = lax.broadcasted_iota(jnp.int32, (tokens, tokens), 1)
    earlier = jnp.where(col < row, 1.0, 0.0).astype(BF16)
    rank = jnp.dot(earlier, named.astype(BF16), preferred_element_type=F32).astype(jnp.int32)
    slot_lane = lax.broadcasted_iota(jnp.int32, (tokens, PAD), 1)
    for j in range(SRC):
        lo, hi = slice(2 * j, 2 * j + 1), slice(2 * j + 1, 2 * j + 2)
        rank_j = jnp.where(par == 0, rank[:, lo], rank[:, hi])
        named_j = jnp.where(par == 0, named[:, lo], named[:, hi])
        gates[j] = jnp.where(par == 0, share[:, lo], share[:, hi])
        onehot[j] = jnp.where(slot_lane == rank_j, named_j, 0.0).astype(BF16)
    mass[pl.ds(y, 1)] = jnp.broadcast_to(jnp.sum(weight, axis=0, keepdims=True), (8, 128))[None]

    pl.semaphore_wait(barrier, len(peers))

    swap = remote(tok, tokx, tok_sem.at[0], tok_sem.at[1], partner)
    swap.start()
    place_r = lax.broadcasted_iota(jnp.int32, (feat, width), 0)
    place_c = lax.broadcasted_iota(jnp.int32, (feat, width), 1)
    mine = jnp.where(place_c == place_r + feat * xl, 1.0, 0.0).astype(BF16)
    other = jnp.where(place_c == place_r + feat * (1 - xl), 1.0, 0.0).astype(BF16)
    wide_v = jnp.dot(tok[...], mine, preferred_element_type=F32)
    swap.wait_recv()
    wide[...] = (wide_v + jnp.dot(tokx[...], other, preferred_element_type=F32)).astype(BF16)

    def to_expert(j):
        return remote(
            slots.at[j], landing.at[me_half], y_send.at[j], y_recv.at[me_half], {"expert": 2 * j + par}
        )

    def from_source(j):
        return remote(slots.at[j], landing.at[j], y_send.at[j], y_recv.at[j], {"expert": 2 * j + par})

    for j in range(SRC):
        block = lax.dot_general(
            onehot[j], wide[...], (((0,), (0,)), ((), ())), preferred_element_type=F32
        ).astype(BF16)
        slots[j] = block

        @pl.when(2 * j + par != y)
        def _():
            to_expert(j).start()

        @pl.when(2 * j + par == y)
        def _():
            landing[j] = block

    def mass_copy(i, slot):
        return remote(
            mass.at[y], mass.at[slot], ms_send.at[i], ms_recv.at[slot], {"expert": lax.rem(y + i + 1, NY)}
        )

    @pl.loop(0, NY - 1)
    def _(i):
        mass_copy(i, y).start()

    parts = []
    for j in range(SRC):

        @pl.when(2 * j + par != y)
        def _():
            from_source(j).wait_recv()

        parts.append(landing[j].astype(F32)[:CAP])
    gath[pl.ds(z, 1), pl.ds(0, HALF)] = jnp.concatenate(parts, axis=0).astype(BF16)[None]

    rows_a, rows_b = pl.ds(0, A), pl.ds(BLO, B)

    def ring(part, way, hop, chunk):
        rows = (rows_a, rows_b)[part]
        return remote(
            gath.at[chunk, rows], gath.at[chunk, rows],
            g_send.at[part, way, hop - 1], g_recv.at[part, way, hop - 1], (ahead, behind)[way],
        )

    def over_x(chunk):
        return remote(
            gath.at[chunk, rows_a], gath.at[chunk, pl.ds(P2, A)],
            xf_send.at[chunk], xf_recv.at[chunk], partner,
        )

    own = remote(
        gath.at[z, pl.ds(A, OWN1)], gath.at[z, pl.ds(P1, OWN1)], own_send, own_recv, partner
    )
    own.start()
    ring(0, 0, 1, z).start()
    ring(0, 1, 1, z).start()
    over_x(z).start()
    own.wait_recv()
    ring(1, 0, 1, z).start()
    ring(1, 1, 1, z).start()
    for load in loads:
        load.wait()
    acc_g[...] = jnp.zeros_like(acc_g)
    acc_u[...] = jnp.zeros_like(acc_u)

    def use(chunk):
        over_x(chunk).wait_recv()
        depth = pl.ds(pl.multiple_of(chunk * width, width), width)

        @pl.loop(0, 2)
        def _(i):
            rows = pl.ds(pl.multiple_of(i * HALF, HALF), HALF)
            block = gath[chunk, rows]
            acc_g[rows] += jnp.dot(block, wg[depth], preferred_element_type=F32)
            acc_u[rows] += jnp.dot(block, wu[depth], preferred_element_type=F32)

    @pl.loop(1, 5)
    def _(hop):
        from_back, from_front = at(-hop), at(hop)

        def arrive(part, way, most, chunk):
            @pl.when(hop <= most)
            def _():
                ring(part, way, hop, chunk).wait_recv()

                @pl.when(hop < most)
                def _():
                    ring(part, way, hop + 1, chunk).start()

                if part == 0:
                    over_x(chunk).start()

        arrive(0, 0, 4, from_back)
        arrive(0, 1, 3, from_front)

        @pl.loop(0, jnp.where(hop == 1, 1, 2))
        def _(i):
            use(at((hop - 1) * (2 * i - 1)))

        arrive(1, 0, 3, from_back)
        arrive(1, 1, 4, from_front)

    use(at(4))

    @pl.loop(0, 2)
    def _(i):
        rows = pl.ds(pl.multiple_of(i * HALF, HALF), HALF)
        gate = acc_g[rows]
        hid[rows] = (gate / (1.0 + jnp.exp(-gate)) * acc_u[rows]).astype(BF16)

    def product(rows, dest):
        cols = pl.ds(pl.multiple_of(dest * width, width), width)
        return jnp.dot(hid[rows], wd[:, cols], preferred_element_type=F32)

    def x_sum(dest):
        return remote(xs.at[dest], xr.at[dest], xs_send.at[dest], xs_recv.at[dest], partner)

    def give_x(i):
        away = (8 - i) // 2
        dest = at(away * (1 - 2 * lax.rem(i, 2)))
        xs[pl.ds(dest, 1)] = product(pl.ds(P2, A), dest).astype(BF16)[None]
        x_sum(dest).start()

    def sums(part, way, hop):
        slot = way * 4 + hop - 1
        src, dst = ((sa, ra), (sb, rb))[part]
        return remote(
            src.at[slot], dst.at[slot],
            r_send.at[part, way, hop - 1], r_recv.at[part, way, hop - 1], (ahead, behind)[way],
        )

    def pass_on(part, way, hop, most, first):
        dest = at((most + 1 - hop) * (1 - 2 * way))
        value = product((rows_a, rows_b)[part], dest)
        if part == 0:
            x_sum(dest).wait_recv()
            value = value + xr[dest].astype(F32)
        slot = way * 4 + hop - 1
        src, dst = ((sa, ra), (sb, rb))[part]
        if not first:
            sums(part, way, hop - 1).wait_recv()
            value = value + dst[slot - 1].astype(F32)
        src[pl.ds(slot, 1)] = value.astype(BF16)[None]
        sums(part, way, hop).start()

    @pl.loop(0, 2)
    def _(i):
        give_x(i)

    pass_on(1, 1, 1, 4, True)
    pass_on(1, 0, 1, 3, True)

    @pl.loop(2, 8)
    def _(i):
        give_x(i)

    pass_on(0, 0, 1, 4, True)
    pass_on(0, 1, 1, 3, True)

    @pl.loop(0, NY - 1)
    def _(i):
        mass_copy(i, lax.rem(y + i + 1, NY)).wait_recv()

    total = mass[0]
    for i in range(1, NY):
        total = total + mass[i]
    bfly[0] = total

    def pair_copy(i):
        return remote(
            bfly.at[2 * i], bfly.at[2 * i + 1], bf_send.at[i], bf_recv.at[i], {"dp": flip(2**i)}
        )

    pair_copy(0).start()

    @pl.loop(2, 5)
    def _(hop):
        pass_on(1, 1, hop, 4, False)

        @pl.when(hop <= 3)
        def _():
            pass_on(1, 0, hop, 3, False)

        pass_on(0, 0, hop, 4, False)

        @pl.when(hop <= 3)
        def _():
            pass_on(0, 1, hop, 3, False)

    for i in (1, 2):
        pair_copy(i - 1).wait_recv()
        bfly[2 * i] = bfly[2 * i - 2] + bfly[2 * i - 1]
        pair_copy(i).start()

    value_b = product(rows_b, z)
    sums(1, 0, 3).wait_recv()
    value_b = value_b + rb[2].astype(F32)
    sums(1, 1, 4).wait_recv()
    value_b = value_b + rb[7].astype(F32)
    cross_s[...] = value_b[OWN1:].astype(BF16)
    crossing = remote(cross_s, cross_r, cr_sem.at[0], cr_sem.at[1], partner)
    crossing.start()
    x_sum(z).wait_recv()
    value_a = product(rows_a, z) + xr[z].astype(F32)
    sums(0, 1, 3).wait_recv()
    value_a = value_a + ra[6].astype(F32)
    sums(0, 0, 4).wait_recv()
    value_a = value_a + ra[3].astype(F32)
    crossing.wait_recv()
    value_b = value_b[:OWN1] + cross_r[...].astype(F32)
    done = jnp.concatenate([value_a, value_b], axis=0)

    def to_source(j):
        return remote(
            back_s.at[j], back_r.at[me_half], bk_send.at[j], bk_recv.at[me_half], {"expert": 2 * j + par}
        )

    def from_expert(j):
        return remote(back_s.at[j], back_r.at[j], bk_send.at[j], bk_recv.at[j], {"expert": 2 * j + par})

    for j in range(SRC):
        block = jnp.concatenate(
            [done[j * CAP : (j + 1) * CAP], jnp.zeros((PAD - CAP, width), F32)], axis=0
        ).astype(BF16)
        back_s[j] = block

        @pl.when(2 * j + par != y)
        def _():
            to_source(j).start()

        @pl.when(2 * j + par == y)
        def _():
            back_r[j] = block

    mixed = jnp.zeros((tokens, width), F32)
    for j in range(SRC):

        @pl.when(2 * j + par != y)
        def _():
            from_expert(j).wait_recv()

        mixed = mixed + gates[j] * jnp.dot(onehot[j], back_r[j], preferred_element_type=F32)
    left, right = mixed[:, :feat], mixed[:, feat:]
    mix_s[...] = jnp.where(xl == 0, right, left).astype(BF16)
    mixing = remote(mix_s, mix_r, mx_sem.at[0], mx_sem.at[1], partner)
    mixing.start()

    pair_copy(2).wait_recv()
    every = (bfly[4] + bfly[5])[0:1] * (1.0 / (tokens * 64))
    bal[...] = NY * jnp.sum(every * every, axis=1, keepdims=True)

    swap.wait_send()
    own.wait_send()
    crossing.wait_send()
    for j in range(SRC):

        @pl.when(2 * j + par != y)
        def _():
            to_expert(j).wait_send()
            to_source(j).wait_send()

    @pl.loop(0, NY - 1)
    def _(i):
        mass_copy(i, y).wait_send()

    @pl.loop(0, NZ)
    def _(i):
        over_x(i).wait_send()
        x_sum(i).wait_send()

    for i in range(3):
        pair_copy(i).wait_send()

    @pl.loop(1, 5)
    def _(hop):
        ring(0, 0, hop, z).wait_send()
        ring(1, 1, hop, z).wait_send()
        sums(0, 0, hop).wait_send()
        sums(1, 1, hop).wait_send()

        @pl.when(hop <= 3)
        def _():
            ring(0, 1, hop, z).wait_send()
            ring(1, 0, hop, z).wait_send()
            sums(0, 1, hop).wait_send()
            sums(1, 0, hop).wait_send()

    mixing.wait_recv()
    out[...] = (jnp.where(xl == 0, left, right) + mix_r[...].astype(F32)).astype(BF16)
    mixing.wait_send()


def body(tokens, expert_ids, gate_raw, w_gate, w_up, w_down):
    count, feat = tokens.shape
    _, model, hidden = w_gate.shape
    width = 2 * feat
    vmem = pl.BlockSpec(memory_space=pltpu.VMEM)
    hbm = pl.BlockSpec(memory_space=pl.ANY)
    dma = pltpu.SemaphoreType.DMA
    mixed, balance = pl.pallas_call(
        kernel,
        out_shape=(
            jax.ShapeDtypeStruct((count, feat), BF16),
            jax.ShapeDtypeStruct((1, 1), F32),
        ),
        in_specs=[vmem, vmem, vmem, hbm, hbm, hbm],
        out_specs=(vmem, vmem),
        scratch_shapes=[
            pltpu.VMEM((model, hidden), BF16),
            pltpu.VMEM((model, hidden), BF16),
            pltpu.VMEM((hidden, model), BF16),
            pltpu.VMEM((count, feat), BF16),
            pltpu.VMEM((count, width), BF16),
            pltpu.VMEM((SRC, count, PAD), BF16),
            pltpu.VMEM((SRC, count, 1), F32),
            pltpu.VMEM((SRC, PAD, width), BF16),
            pltpu.VMEM((SRC, PAD, width), BF16),
            pltpu.VMEM((NZ, ROWS, width), BF16),
            pltpu.VMEM((ROWS, hidden), F32),
            pltpu.VMEM((ROWS, hidden), F32),
            pltpu.VMEM((ROWS, hidden), BF16),
            pltpu.VMEM((8, A, width), BF16),
            pltpu.VMEM((8, B, width), BF16),
            pltpu.VMEM((8, A, width), BF16),
            pltpu.VMEM((8, B, width), BF16),
            pltpu.VMEM((NZ, A, width), BF16),
            pltpu.VMEM((NZ, A, width), BF16),
            pltpu.VMEM((OWN1, width), BF16),
            pltpu.VMEM((OWN1, width), BF16),
            pltpu.VMEM((SRC, PAD, width), BF16),
            pltpu.VMEM((SRC, PAD, width), BF16),
            pltpu.VMEM((count, feat), BF16),
            pltpu.VMEM((count, feat), BF16),
            pltpu.VMEM((NY, 8, 128), F32),
            pltpu.VMEM((6, 8, 128), F32),
            dma((3,)),
            dma((2,)),
            dma((SRC,)),
            dma((SRC,)),
            dma(()),
            dma(()),
            dma((2, 2, 4)),
            dma((2, 2, 4)),
            dma((NZ,)),
            dma((NZ,)),
            dma((2, 2, 4)),
            dma((2, 2, 4)),
            dma((NZ,)),
            dma((NZ,)),
            dma((2,)),
            dma((SRC,)),
            dma((SRC,)),
            dma((2,)),
            dma((NY,)),
            dma((NY,)),
            dma((3,)),
            dma((3,)),
        ],
        compiler_params=pltpu.CompilerParams(
            collective_id=0, has_side_effects=True, vmem_limit_bytes=48 * 1024 * 1024
        ),
    )(tokens, expert_ids, gate_raw, w_gate, w_up, w_down)
    return (mixed, balance.reshape(()))


def solution(mesh):
    return jax.shard_map(
        body,
        mesh=mesh,
        in_specs=(
            P(("dp", "expert"), "tensor"),
            P(("dp", "expert"), None),
            P(("dp", "expert"), None),
            P("expert", None, "tensor"),
            P("expert", None, "tensor"),
            P("expert", "tensor", None),
        ),
        out_specs=(P(("dp", "expert"), "tensor"), P()),
        check_vma=False,
    )
```

time: 394 us -> 123 us (0.31)
  the two profiles are of different devices: /device:TPU:16 before, /device:TPU:32 now
where the time goes in v1:
time: 123 us; the launch traced here: 122 us
  Pallas kernels  108 us (88%)
  local copies, waits for them, and re-layouts  11.9 us (10%)
  between operations  2.47 us (2%)
    pallas_call x1, Pallas kernels, body(): pl.pallas_call(kernel, out_shape=(jax.ShapeDtypeStruct((count, feat), BF1...  108 us
    unnamed x8, local copies, waits for them, and re-layouts  11.9 us

profile of v1, /device:TPU:32, one launch (start us, length us, event | category | flops | bytes accessed | tf_op | source)
XLA Modules:
  0.0 122.2 jit_solution(10134944451731802422)
XLA Ops:
  0.6 0.9 copy.8.tok
  1.5 0.8 copy.9.ids
  2.3 0.8 copy.10.raw
  3.1 2.9 %copy.11.wg_hbm = bf16[1,3072,336]{2,1,0:T(8,128)(2,1)S(1)} copy(bf16[1,3072,336]{1,2,0:T(8,128)(2,1)} %param.9) | data formatting | bytes 4128768 | tf_op args[3]
  6.0 4.2 %copy.12.wu_hbm = bf16[1,3072,336]{2,1,0:T(8,128)(2,1)} copy(bf16[1,3072,336]{1,2,0:T(8,128)(2,1)} %param.10) | data formatting | bytes 4128768 | tf_op args[4]
  10.2 0.0 copy-start
  10.2 1.6 %copy-done = bf16[1,336,3072]{2,1,0:T(8,128)(2,1)S(1)} copy-done((bf16[1,336,3072]{2,1,0:T(8,128)(2,1)S(1)}, bf16[1,336,3072]{2,1,0:T(8,128)(2,1)}, u32[]{:S(2)}) %copy-start) | copy-done | bytes 2064408
  11.8 107.9 %shard_map.77 = (bf16[128,192]{1,0:T(8,128)(2,1)S(1)}, f32[1,1]{1,0:T(1,128)}) custom-call(bf16[128,192]{1,0:T(8,128)(2,1)S(1)} %copy.8.tok, s32[128,4]{1,0:T(8,128)S(1)} %copy.9.ids, f32[128,4]{1,0:T(8,128)S(1)} %copy.10.raw, bf16[1,3072,336]{2,1,0:T(8,128)(2,1)S(1)} %copy.11.wg_hbm, bf16[1,3072,336]{2,1,0:T(8,128)(2,1)} %copy.12.wu_hbm, ...), custom_call_target="tpu_custom_call" | custom-call | tf_op jit(solution)/shard_map/pallas_call | solution.py:416
  119.7 0.7 copy.13
Async XLA Ops:
  10.2 1.6 %copy-start = (bf16[1,336,3072]{2,1,0:T(8,128)(2,1)S(1)}, bf16[1,336,3072]{2,1,0:T(8,128)(2,1)}, u32[]{:S(2)}) copy-start(bf16[1,336,3072]{2,1,0:T(8,128)(2,1)} %wd_hbm.1) | copy-start | bytes 6193156

commit v2 on v1

--- a/solution.py
+++ b/solution.py
@@ -35,14 +35,14 @@
 
 def kernel(
     tok, ids, raw, wg_hbm, wu_hbm, wd_hbm, out, bal,
-    wg, wu, wd, tokx, wide, onehot, gates, slots, landing, gath, acc_g, acc_u, hid,
+    wg, wu, wd, wide, onehot, gates, slots, landing, gath, acc_g, acc_u, hid,
     sa, sb, ra, rb, xs, xr, cross_s, cross_r, back_s, back_r, mix_s, mix_r, mass, bfly,
     w_sem, tok_sem, y_send, y_recv, own_send, own_recv,
     g_send, g_recv, xf_send, xf_recv, r_send, r_recv, xs_send, xs_recv,
     cr_sem, bk_send, bk_recv, mx_sem, ms_send, ms_recv, bf_send, bf_recv,
 ):
     dp, ten, y = lax.axis_index("dp"), lax.axis_index("tensor"), lax.axis_index("expert")
-    tokens, feat = tok.shape
+    feat, tokens = tok.shape
     width = 2 * feat
     z, xl = ten // 2, lax.rem(ten, 2)
     turn = 1 - 2 * lax.rem(dp, 2)
@@ -72,41 +72,38 @@
     for peer in peers:
         pl.semaphore_signal(barrier, inc=1, device_id=peer, device_id_type=MESH)
 
-    lane = lax.broadcasted_iota(jnp.int32, (tokens, 128), 1)
+    expert = lax.broadcasted_iota(jnp.int32, (16, tokens), 0)
     ids_v, raw_v = ids[...], raw[...]
-    norm_v = raw_v / jnp.sum(raw_v, axis=1, keepdims=True)
-    named = jnp.zeros((tokens, 128), F32)
-    weight = jnp.zeros((tokens, 128), F32)
-    share = jnp.zeros((tokens, 128), F32)
-    for k in range(ids.shape[1]):
-        hit = ids_v[:, k : k + 1] == lane
+    norm_v = raw_v / jnp.sum(raw_v, axis=0, keepdims=True)
+    named = jnp.zeros((16, tokens), F32)
+    weight = jnp.zeros((16, tokens), F32)
+    share = jnp.zeros((16, tokens), F32)
+    for k in range(ids.shape[0]):
+        hit = ids_v[k : k + 1] == expert
         named = jnp.where(hit, 1.0, named)
-        weight = jnp.where(hit, raw_v[:, k : k + 1], weight)
-        share = jnp.where(hit, norm_v[:, k : k + 1], share)
+        weight = jnp.where(hit, raw_v[k : k + 1], weight)
+        share = jnp.where(hit, norm_v[k : k + 1], share)
     row = lax.broadcasted_iota(jnp.int32, (tokens, tokens), 0)
     col = lax.broadcasted_iota(jnp.int32, (tokens, tokens), 1)
-    earlier = jnp.where(col < row, 1.0, 0.0).astype(BF16)
-    rank = jnp.dot(earlier, named.astype(BF16), preferred_element_type=F32).astype(jnp.int32)
-    slot_lane = lax.broadcasted_iota(jnp.int32, (tokens, PAD), 1)
+    earlier = jnp.where(row < col, 1.0, 0.0).astype(BF16)
+    rank = jnp.dot(named.astype(BF16), earlier, preferred_element_type=F32).astype(jnp.int32)
+    slot = lax.broadcasted_iota(jnp.int32, (PAD, tokens), 0)
     for j in range(SRC):
         lo, hi = slice(2 * j, 2 * j + 1), slice(2 * j + 1, 2 * j + 2)
-        rank_j = jnp.where(par == 0, rank[:, lo], rank[:, hi])
-        named_j = jnp.where(par == 0, named[:, lo], named[:, hi])
-        gates[j] = jnp.where(par == 0, share[:, lo], share[:, hi])
-        onehot[j] = jnp.where(slot_lane == rank_j, named_j, 0.0).astype(BF16)
-    mass[pl.ds(y, 1)] = jnp.broadcast_to(jnp.sum(weight, axis=0, keepdims=True), (8, 128))[None]
+        rank_j = jnp.where(par == 0, rank[lo], rank[hi])
+        named_j = jnp.where(par == 0, named[lo], named[hi])
+        gates[j] = jnp.where(par == 0, share[lo], share[hi])
+        onehot[j] = jnp.where(slot == rank_j, named_j, 0.0).astype(BF16)
+    mass[pl.ds(y, 1)] = jnp.broadcast_to(jnp.sum(weight[:NY], axis=1, keepdims=True), (NY, 128))[None]
 
     pl.semaphore_wait(barrier, len(peers))
 
-    swap = remote(tok, tokx, tok_sem.at[0], tok_sem.at[1], partner)
+    swap = remote(
+        tok, wide.at[pl.ds(pl.multiple_of(xl * feat, feat), feat)], tok_sem.at[0], tok_sem.at[1], partner
+    )
     swap.start()
-    place_r = lax.broadcasted_iota(jnp.int32, (feat, width), 0)
-    place_c = lax.broadcasted_iota(jnp.int32, (feat, width), 1)
-    mine = jnp.where(place_c == place_r + feat * xl, 1.0, 0.0).astype(BF16)
-    other = jnp.where(place_c == place_r + feat * (1 - xl), 1.0, 0.0).astype(BF16)
-    wide_v = jnp.dot(tok[...], mine, preferred_element_type=F32)
+    wide[pl.ds(pl.multiple_of(xl * feat, feat), feat)] = tok[...]
     swap.wait_recv()
-    wide[...] = (wide_v + jnp.dot(tokx[...], other, preferred_element_type=F32)).astype(BF16)
 
     def to_expert(j):
         return remote(
@@ -118,7 +115,7 @@
 
     for j in range(SRC):
         block = lax.dot_general(
-            onehot[j], wide[...], (((0,), (0,)), ((), ())), preferred_element_type=F32
+            onehot[j], wide[...], (((1,), (1,)), ((), ())), preferred_element_type=F32
         ).astype(BF16)
         slots[j] = block
 
@@ -187,8 +184,10 @@
         def _(i):
             rows = pl.ds(pl.multiple_of(i * HALF, HALF), HALF)
             block = gath[chunk, rows]
-            acc_g[rows] += jnp.dot(block, wg[depth], preferred_element_type=F32)
-            acc_u[rows] += jnp.dot(block, wu[depth], preferred_element_type=F32)
+            for acc, weights in ((acc_g, wg), (acc_u, wu)):
+                acc[rows] += lax.dot_general(
+                    block, weights[:, depth], (((1,), (1,)), ((), ())), preferred_element_type=F32
+                )
 
     @pl.loop(1, 5)
     def _(hop):
@@ -348,22 +347,24 @@
         def _():
             back_r[j] = block
 
-    mixed = jnp.zeros((tokens, width), F32)
+    mixed = jnp.zeros((width, tokens), F32)
     for j in range(SRC):
 
         @pl.when(2 * j + par != y)
         def _():
             from_expert(j).wait_recv()
 
-        mixed = mixed + gates[j] * jnp.dot(onehot[j], back_r[j], preferred_element_type=F32)
-    left, right = mixed[:, :feat], mixed[:, feat:]
+        mixed = mixed + gates[j] * lax.dot_general(
+            back_r[j], onehot[j], (((0,), (0,)), ((), ())), preferred_element_type=F32
+        )
+    left, right = mixed[:feat], mixed[feat:]
     mix_s[...] = jnp.where(xl == 0, right, left).astype(BF16)
     mixing = remote(mix_s, mix_r, mx_sem.at[0], mx_sem.at[1], partner)
     mixing.start()
 
     pair_copy(2).wait_recv()
-    every = (bfly[4] + bfly[5])[0:1] * (1.0 / (tokens * 64))
-    bal[...] = NY * jnp.sum(every * every, axis=1, keepdims=True)
+    every = (bfly[4] + bfly[5]) * (1.0 / (tokens * 64))
+    bal[...] = NY * jnp.sum(every * every, axis=0, keepdims=True)[:, :1]
 
     swap.wait_send()
     own.wait_send()
@@ -409,6 +410,7 @@
 def body(tokens, expert_ids, gate_raw, w_gate, w_up, w_down):
     count, feat = tokens.shape
     _, model, hidden = w_gate.shape
+    turned = [jnp.swapaxes(v, -1, -2) for v in (tokens, expert_ids, gate_raw, w_gate, w_up)]
     width = 2 * feat
     vmem = pl.BlockSpec(memory_space=pltpu.VMEM)
     hbm = pl.BlockSpec(memory_space=pl.ANY)
@@ -416,19 +418,18 @@
     mixed, balance = pl.pallas_call(
         kernel,
         out_shape=(
-            jax.ShapeDtypeStruct((count, feat), BF16),
+            jax.ShapeDtypeStruct((feat, count), BF16),
             jax.ShapeDtypeStruct((1, 1), F32),
         ),
         in_specs=[vmem, vmem, vmem, hbm, hbm, hbm],
         out_specs=(vmem, vmem),
         scratch_shapes=[
-            pltpu.VMEM((model, hidden), BF16),
-            pltpu.VMEM((model, hidden), BF16),
             pltpu.VMEM((hidden, model), BF16),
-            pltpu.VMEM((count, feat), BF16),
-            pltpu.VMEM((count, width), BF16),
-            pltpu.VMEM((SRC, count, PAD), BF16),
-            pltpu.VMEM((SRC, count, 1), F32),
+            pltpu.VMEM((hidden, model), BF16),
+            pltpu.VMEM((hidden, model), BF16),
+            pltpu.VMEM((width, count), BF16),
+            pltpu.VMEM((SRC, PAD, count), BF16),
+            pltpu.VMEM((SRC, 1, count), F32),
             pltpu.VMEM((SRC, PAD, width), BF16),
             pltpu.VMEM((SRC, PAD, width), BF16),
             pltpu.VMEM((NZ, ROWS, width), BF16),
@@ -445,8 +446,8 @@
             pltpu.VMEM((OWN1, width), BF16),
             pltpu.VMEM((SRC, PAD, width), BF16),
             pltpu.VMEM((SRC, PAD, width), BF16),
-            pltpu.VMEM((count, feat), BF16),
-            pltpu.VMEM((count, feat), BF16),
+            pltpu.VMEM((feat, count), BF16),
+            pltpu.VMEM((feat, count), BF16),
             pltpu.VMEM((NY, 8, 128), F32),
             pltpu.VMEM((6, 8, 128), F32),
             dma((3,)),
@@ -473,10 +474,10 @@
             dma((3,)),
         ],
         compiler_params=pltpu.CompilerParams(
-            collective_id=0, has_side_effects=True, vmem_limit_bytes=48 * 1024 * 1024
+            collective_id=0, has_side_effects=True, vmem_limit_bytes=60 * 1024 * 1024
         ),
-    )(tokens, expert_ids, gate_raw, w_gate, w_up, w_down)
-    return (mixed, balance.reshape(()))
+    )(*turned, w_down)
+    return (mixed.T, balance.reshape(()))
 
 
 def solution(mesh):

time: 123 us -> 112 us (0.911)
  the two profiles are of different devices: /device:TPU:32 before, /device:TPU:16 now
where the time goes in v2:
time: 112 us; the launch traced here: 111 us
  Pallas kernels  108 us (96%)
  between operations  2.38 us (2%)
  local copies, waits for them, and re-layouts  1.42 us (1%)
    pallas_call x1, Pallas kernels, body(): pl.pallas_call(kernel, out_shape=(jax.ShapeDtypeStruct((feat, count), BF1...  108 us

profile of v2, /device:TPU:16, one launch (start us, length us, event | category | flops | bytes accessed | tf_op | source)
XLA Modules:
  0.0 111.5 jit_solution(3219849657258778967)
XLA Ops:
  0.6 107.7 %shard_map.77 = (bf16[192,128]{1,0:T(8,128)(2,1)}, f32[1,1]{1,0:T(1,128)}) custom-call(bf16[192,128]{1,0:T(8,128)(2,1)} %bitcast.9, s32[4,128]{1,0:T(4,128)} %bitcast.11, f32[4,128]{1,0:T(4,128)} %bitcast.12, bf16[1,336,3072]{2,1,0:T(8,128)(2,1)} %bitcast.7, bf16[1,336,3072]{2,1,0:T(8,128)(2,1)} %bitcast.8, bf16[1,336,3072]{2,1,0:T(8,128)(2,1)} %wd_hbm.1), custom_call_target="tpu_custom_call" | custom-call | tf_op jit(solution)/shard_map/pallas_call | solution.py:418
  108.3 1.4 %copy.10 = bf16[128,192]{0,1:T(8,128)(2,1)} copy(bf16[128,192]{0,1:T(8,128)(2,1)} %bitcast.10) | data formatting | bytes 98304

commit v3 on v2

v3 whole, which is shorter than its diff:
```python
import functools

import jax
import jax.numpy as jnp
from jax import lax
from jax.experimental import pallas as pl
from jax.experimental.pallas import tpu as pltpu
from jax.sharding import PartitionSpec as P

MESH = pl.DeviceIdType.MESH
F32 = jnp.float32
BF16 = jnp.bfloat16

NZ = 8
NY = 8
CAP = 72
PAD = 80
SRC = 4
PART = 2 * CAP
ROWS = 4 * PART
NEAR, FAR, FAR_X, NEAR_X = 0, PART, 2 * PART, 3 * PART
ROUND = (NEAR, FAR_X, FAR)
MOST = ((4, 3), (3, 4), (3, 4))


def remote(src, dst, send, recv, device):
    return pltpu.make_async_remote_copy(
        src_ref=src,
        dst_ref=dst,
        send_sem=send,
        recv_sem=recv,
        device_id=device,
        device_id_type=MESH,
    )


def kernel(
    tok, ids, raw, wg_hbm, wu_hbm, wd_hbm, out, bal,
    wg, wu, wd, wide, onehot, gates, slots, landing, gath, acc_g, acc_u, hid,
    sums_s, sums_r, xs, xr, cross_s, cross_r, back_s, back_r, mix_s, mix_r, mass, bfly,
    w_sem, tok_sem, y_send, y_recv, own_send, own_recv,
    g_send, g_recv, xf_send, xf_recv, r_send, r_recv, xs_send, xs_recv,
    cr_sem, bk_send, bk_recv, mx_sem, ms_send, ms_recv, bf_send, bf_recv,
):
    dp, ten, y = lax.axis_index("dp"), lax.axis_index("tensor"), lax.axis_index("expert")
    feat, tokens = tok.shape
    width = 2 * feat
    z, xl = ten // 2, lax.rem(ten, 2)
    turn = 1 - 2 * lax.rem(dp, 2)
    steps_y = (2 * xl, 1 - 3 * xl, 4 * xl - 1, 4 - 7 * xl)

    def at(steps):
        return lax.rem(z + turn * steps + 2 * NZ, NZ)

    partner = {"tensor": z * 2 + 1 - xl}
    ahead = {"tensor": at(1) * 2 + xl}
    behind = {"tensor": at(-1) * 2 + xl}

    def along_y(steps):
        return lax.rem(y + steps + NY, NY)

    def unless_own(j, act):
        if j == 0:
            pl.when(xl == 1)(act)
        else:
            act()

    def flip(bit):
        return dp + bit - 2 * bit * lax.rem(dp // bit, 2)

    loads = [
        pltpu.make_async_copy(src.at[0], dst, w_sem.at[i])
        for i, (src, dst) in enumerate(((wg_hbm, wg), (wu_hbm, wu), (wd_hbm, wd)))
    ]
    for load in loads:
        load.start()

    barrier = pltpu.get_barrier_semaphore()
    peers = [{"expert": lax.rem(y + i, NY)} for i in range(1, NY)]
    peers += [partner, ahead, behind] + [{"dp": flip(bit)} for bit in (1, 2, 4)]
    for peer in peers:
        pl.semaphore_signal(barrier, inc=1, device_id=peer, device_id_type=MESH)

    expert = lax.broadcasted_iota(jnp.int32, (16, tokens), 0)
    ids_v, raw_v = ids[...], raw[...]
    norm_v = raw_v / jnp.sum(raw_v, axis=0, keepdims=True)
    named = jnp.zeros((16, tokens), F32)
    weight = jnp.zeros((16, tokens), F32)
    share = jnp.zeros((16, tokens), F32)
    for k in range(ids.shape[0]):
        hit = ids_v[k : k + 1] == expert
        named = jnp.where(hit, 1.0, named)
        weight = jnp.where(hit, raw_v[k : k + 1], weight)
        share = jnp.where(hit, norm_v[k : k + 1], share)
    row = lax.broadcasted_iota(jnp.int32, (tokens, tokens), 0)
    col = lax.broadcasted_iota(jnp.int32, (tokens, tokens), 1)
    earlier = jnp.where(row < col, 1.0, 0.0).astype(BF16)
    rank = jnp.dot(named.astype(BF16), earlier, preferred_element_type=F32).astype(jnp.int32)
    rank = jnp.where(named > 0, rank, -1)
    slot = lax.broadcasted_iota(jnp.int32, (PAD, tokens), 0)
    for j in range(SRC):
        this = expert == along_y(steps_y[j])
        rank_j = jnp.sum(jnp.where(this, rank, 0), axis=0, keepdims=True)
        gates[j] = jnp.sum(jnp.where(this, share, 0.0), axis=0, keepdims=True)
        onehot[j] = jnp.where(slot == rank_j, 1.0, 0.0).astype(BF16)
    mass[pl.ds(y, 1)] = jnp.broadcast_to(jnp.sum(weight[:NY], axis=1, keepdims=True), (NY, 128))[None]

    pl.semaphore_wait(barrier, len(peers))

    swap = remote(
        tok, wide.at[pl.ds(pl.multiple_of(xl * feat, feat), feat)], tok_sem.at[0], tok_sem.at[1], partner
    )
    swap.start()
    wide[pl.ds(pl.multiple_of(xl * feat, feat), feat)] = tok[...]
    swap.wait_recv()

    def to_expert(j):
        return remote(
            slots.at[j], landing.at[j], y_send.at[j], y_recv.at[j], {"expert": along_y(steps_y[j])}
        )

    for j in range(SRC):
        slots[j] = lax.dot_general(
            onehot[j], wide[...], (((1,), (1,)), ((), ())), preferred_element_type=F32
        ).astype(BF16)
        unless_own(j, to_expert(j).start)

    @pl.when(xl == 0)
    def _():
        landing[0] = slots[0]

    def mass_copy(i, slot):
        return remote(
            mass.at[y], mass.at[slot], ms_send.at[i], ms_recv.at[slot], {"expert": lax.rem(y + i + 1, NY)}
        )

    def land(j, first):
        unless_own(j, to_expert(j).wait_recv)
        unless_own(j + 1, to_expert(j + 1).wait_recv)
        both = [landing[i].astype(F32)[:CAP] for i in (j, j + 1)]
        gath[pl.ds(z, 1), pl.ds(first, PART)] = jnp.concatenate(both, axis=0).astype(BF16)[None]

    def ring(part, way, hop, chunk):
        rows = pl.ds(ROUND[part], PART)
        return remote(
            gath.at[chunk, rows], gath.at[chunk, rows],
            g_send.at[part, way, hop - 1], g_recv.at[part, way, hop - 1], (ahead, behind)[way],
        )

    def over_x(chunk):
        return remote(
            gath.at[chunk, pl.ds(NEAR, PART)], gath.at[chunk, pl.ds(NEAR_X, PART)],
            xf_send.at[chunk], xf_recv.at[chunk], partner,
        )

    own = remote(
        gath.at[z, pl.ds(FAR, PART)], gath.at[z, pl.ds(FAR_X, PART)], own_send, own_recv, partner
    )
    land(0, NEAR)
    ring(0, 0, 1, z).start()
    ring(0, 1, 1, z).start()
    over_x(z).start()
    land(2, FAR)
    own.start()
    ring(2, 0, 1, z).start()
    ring(2, 1, 1, z).start()

    @pl.loop(0, NY - 1)
    def _(i):
        mass_copy(i, y).start()

    acc_g[...] = jnp.zeros_like(acc_g)
    acc_u[...] = jnp.zeros_like(acc_u)
    own.wait_recv()
    ring(1, 0, 1, z).start()
    ring(1, 1, 1, z).start()
    for load in loads:
        load.wait()

    def use(chunk, first, count):
        rows = pl.ds(first, count)
        depth = pl.ds(pl.multiple_of(chunk * width, width), width)
        for acc, weights in ((acc_g, wg), (acc_u, wu)):
            acc[rows] += lax.dot_general(
                gath[chunk, rows], weights[:, depth], (((1,), (1,)), ((), ())), preferred_element_type=F32
            )

    def activate(first, count):
        rows = pl.ds(first, count)
        gate = acc_g[rows]
        hid[rows] = (gate / (1.0 + jnp.exp(-gate)) * acc_u[rows]).astype(BF16)

    @pl.loop(1, 5)
    def _(hop):
        chunks = (at(-hop), at(hop))

        def arrive(part, way):
            @pl.when(hop <= MOST[part][way])
            def _():
                ring(part, way, hop, chunks[way]).wait_recv()

                @pl.when(hop < MOST[part][way])
                def _():
                    ring(part, way, hop + 1, chunks[way]).start()

                if part == 0:
                    over_x(chunks[way]).start()

        arrive(0, 0)
        arrive(0, 1)

        @pl.loop(0, jnp.where(hop == 1, 1, 2))
        def _(i):
            chunk = at((hop - 1) * (2 * i - 1))
            over_x(chunk).wait_recv()

            @pl.loop(0, 2)
            def _(half):
                use(chunk, pl.multiple_of(half * 2 * PART, 2 * PART), 2 * PART)

        for part in (2, 1):
            arrive(part, 0)
            arrive(part, 1)

    last = at(4)
    use(last, FAR, 2 * PART)
    activate(FAR, 2 * PART)

    def product(first, dest):
        cols = pl.ds(pl.multiple_of(dest * width, width), width)
        return jnp.dot(hid[pl.ds(first, PART)], wd[:, cols], preferred_element_type=F32)

    def x_sum(dest):
        return remote(xs.at[dest], xr.at[dest], xs_send.at[dest], xs_recv.at[dest], partner)

    def give_x(i):
        away = (8 - i) // 2
        dest = at(away * (1 - 2 * lax.rem(i, 2)))
        xs[pl.ds(dest, 1)] = product(NEAR_X, dest).astype(BF16)[None]
        x_sum(dest).start()

    def sums(part, way, hop):
        slot = way * 4 + hop - 1
        return remote(
            sums_s.at[part, slot], sums_r.at[part, slot],
            r_send.at[part, way, hop - 1], r_recv.at[part, way, hop - 1], (ahead, behind)[way],
        )

    def pass_on(part, way, hop, first=False):
        dest = at((MOST[part][way] + 1 - hop) * (1 - 2 * way))
        value = product(ROUND[part], dest)
        if part == 0:
            x_sum(dest).wait_recv()
            value = value + xr[dest].astype(F32)
        slot = way * 4 + hop - 1
        if not first:
            sums(part, way, hop - 1).wait_recv()
            value = value + sums_r[part, slot - 1].astype(F32)
        sums_s[part, pl.ds(slot, 1)] = value.astype(BF16)[None]
        sums(part, way, hop).start()

    for part in (1, 2):
        for way in (1, 0):
            pass_on(part, way, 1, True)
    over_x(last).wait_recv()
    for first in (NEAR_X, NEAR):
        use(last, first, PART)
        activate(first, PART)

    @pl.loop(0, 8)
    def _(i):
        give_x(i)

    pass_on(0, 0, 1, True)
    pass_on(0, 1, 1, True)

    @pl.loop(0, NY - 1)
    def _(i):
        mass_copy(i, lax.rem(y + i + 1, NY)).wait_recv()

    total = mass[0]
    for i in range(1, NY):
        total = total + mass[i]
    bfly[0] = total

    def pair_copy(i):
        return remote(
            bfly.at[2 * i], bfly.at[2 * i + 1], bf_send.at[i], bf_recv.at[i], {"dp": flip(2**i)}
        )

    pair_copy(0).start()

    @pl.loop(2, 5)
    def _(hop):
        for part in (1, 2, 0):
            for way in range(2):
                pl.when(hop <= MOST[part][way])(functools.partial(pass_on, part, way, hop))

        for i in (1, 2):

            @pl.when(hop == i + 2)
            def _(i=i):
                pair_copy(i - 1).wait_recv()
                bfly[2 * i] = bfly[2 * i - 2] + bfly[2 * i - 1]
                pair_copy(i).start()

    def total_of(part):
        value = product(ROUND[part], z)
        for way in range(2):
            most = MOST[part][way]
            sums(part, way, most).wait_recv()
            value = value + sums_r[part, way * 4 + most - 1].astype(F32)
        return value

    cross_s[...] = total_of(1).astype(BF16)
    crossing = remote(cross_s, cross_r, cr_sem.at[0], cr_sem.at[1], partner)
    crossing.start()

    def to_source(j):
        return remote(
            back_s.at[j], back_r.at[j], bk_send.at[j], bk_recv.at[j], {"expert": along_y(-steps_y[j])}
        )

    def give_back(done, j):
        for i in range(2):
            back_s[j + i] = jnp.concatenate(
                [done[i * CAP : (i + 1) * CAP], jnp.zeros((PAD - CAP, width), F32)], axis=0
            ).astype(BF16)
            unless_own(j + i, to_source(j + i).start)

    x_sum(z).wait_recv()
    give_back(total_of(0) + xr[z].astype(F32), 0)

    @pl.when(xl == 0)
    def _():
        back_r[0] = back_s[0]

    far = total_of(2)
    crossing.wait_recv()
    give_back(far + cross_r[...].astype(F32), 2)

    mixed = jnp.zeros((width, tokens), F32)
    for j in range(SRC):
        unless_own(j, to_source(j).wait_recv)
        mixed = mixed + gates[j] * lax.dot_general(
            back_r[j], onehot[j], (((0,), (0,)), ((), ())), preferred_element_type=F32
        )
    left, right = mixed[:feat], mixed[feat:]
    mix_s[...] = jnp.where(xl == 0, right, left).astype(BF16)
    mixing = remote(mix_s, mix_r, mx_sem.at[0], mx_sem.at[1], partner)
    mixing.start()

    pair_copy(2).wait_recv()
    every = (bfly[4] + bfly[5]) * (1.0 / (tokens * 64))
    bal[...] = NY * jnp.sum(every * every, axis=0, keepdims=True)[:, :1]

    swap.wait_send()
    own.wait_send()
    crossing.wait_send()
    for j in range(SRC):
        unless_own(j, to_expert(j).wait_send)
        unless_own(j, to_source(j).wait_send)

    @pl.loop(0, NY - 1)
    def _(i):
        mass_copy(i, y).wait_send()

    @pl.loop(0, NZ)
    def _(i):
        over_x(i).wait_send()
        x_sum(i).wait_send()

    for i in range(3):
        pair_copy(i).wait_send()

    @pl.loop(1, 5)
    def _(hop):
        for part in range(3):
            for way in range(2):

                def sent(part=part, way=way):
                    ring(part, way, hop, z).wait_send()
                    sums(part, way, hop).wait_send()

                pl.when(hop <= MOST[part][way])(sent)

    mixing.wait_recv()
    out[...] = (jnp.where(xl == 0, left, right) + mix_r[...].astype(F32)).astype(BF16)
    mixing.wait_send()


def body(tokens, expert_ids, gate_raw, w_gate, w_up, w_down):
    count, feat = tokens.shape
    _, model, hidden = w_gate.shape
    turned = [jnp.swapaxes(v, -1, -2) for v in (tokens, expert_ids, gate_raw, w_gate, w_up)]
    width = 2 * feat
    vmem = pl.BlockSpec(memory_space=pltpu.VMEM)
    hbm = pl.BlockSpec(memory_space=pl.ANY)
    dma = pltpu.SemaphoreType.DMA
    mixed, balance = pl.pallas_call(
        kernel,
        out_shape=(
            jax.ShapeDtypeStruct((feat, count), BF16),
            jax.ShapeDtypeStruct((1, 1), F32),
        ),
        in_specs=[vmem, vmem, vmem, hbm, hbm, hbm],
        out_specs=(vmem, vmem),
        scratch_shapes=[
            pltpu.VMEM((hidden, model), BF16),
            pltpu.VMEM((hidden, model), BF16),
            pltpu.VMEM((hidden, model), BF16),
            pltpu.VMEM((width, count), BF16),
            pltpu.VMEM((SRC, PAD, count), BF16),
            pltpu.VMEM((SRC, 1, count), F32),
            pltpu.VMEM((SRC, PAD, width), BF16),
            pltpu.VMEM((SRC, PAD, width), BF16),
            pltpu.VMEM((NZ, ROWS, width), BF16),
            pltpu.VMEM((ROWS, hidden), F32),
            pltpu.VMEM((ROWS, hidden), F32),
            pltpu.VMEM((ROWS, hidden), BF16),
            pltpu.VMEM((3, 8, PART, width), BF16),
            pltpu.VMEM((3, 8, PART, width), BF16),
            pltpu.VMEM((NZ, PART, width), BF16),
            pltpu.VMEM((NZ, PART, width), BF16),
            pltpu.VMEM((PART, width), BF16),
            pltpu.VMEM((PART, width), BF16),
            pltpu.VMEM((SRC, PAD, width), BF16),
            pltpu.VMEM((SRC, PAD, width), BF16),
            pltpu.VMEM((feat, count), BF16),
            pltpu.VMEM((feat, count), BF16),
            pltpu.VMEM((NY, 8, 128), F32),
            pltpu.VMEM((6, 8, 128), F32),
            dma((3,)),
            dma((2,)),
            dma((SRC,)),
            dma((SRC,)),
            dma(()),
            dma(()),
            dma((3, 2, 4)),
            dma((3, 2, 4)),
            dma((NZ,)),
            dma((NZ,)),
            dma((3, 2, 4)),
            dma((3, 2, 4)),
            dma((NZ,)),
            dma((NZ,)),
            dma((2,)),
            dma((SRC,)),
            dma((SRC,)),
            dma((2,)),
            dma((NY,)),
            dma((NY,)),
            dma((3,)),
            dma((3,)),
        ],
        compiler_params=pltpu.CompilerParams(
            collective_id=0, has_side_effects=True, vmem_limit_bytes=60 * 1024 * 1024
        ),
    )(*turned, w_down)
    return (mixed.T, balance.reshape(()))


def solution(mesh):
    return jax.shard_map(
        body,
        mesh=mesh,
        in_specs=(
            P(("dp", "expert"), "tensor"),
            P(("dp", "expert"), None),
            P(("dp", "expert"), None),
            P("expert", None, "tensor"),
            P("expert", None, "tensor"),
            P("expert", "tensor", None),
        ),
        out_specs=(P(("dp", "expert"), "tensor"), P()),
        check_vma=False,
    )
```

time: 112 us -> 108 us (0.964)
  Pallas kernels: 108 us -> 103 us
    pallas_call x1, Pallas kernels: 108 us -> 103 us  [body(): pl.pallas_call(kernel, out_shape=(jax.ShapeDtypeStruct((feat, count), BF1...]
where the time goes in v3:
time: 108 us; the launch traced here: 107 us
  Pallas kernels  103 us (95%)
  between operations  2.38 us (2%)
  local copies, waits for them, and re-layouts  1.42 us (1%)
    pallas_call x1, Pallas kernels, body(): pl.pallas_call(kernel, out_shape=(jax.ShapeDtypeStruct((feat, count), BF1...  103 us

profile of v3, /device:TPU:16, one launch (start us, length us, event | category | flops | bytes accessed | tf_op | source)
XLA Modules:
  0.0 107.3 jit_solution(11090660666080623269)
XLA Ops:
  0.6 103.5 %shard_map.77 = (bf16[192,128]{1,0:T(8,128)(2,1)}, f32[1,1]{1,0:T(1,128)}) custom-call(bf16[192,128]{1,0:T(8,128)(2,1)} %bitcast.9, s32[4,128]{1,0:T(4,128)} %bitcast.11, f32[4,128]{1,0:T(4,128)} %bitcast.12, bf16[1,336,3072]{2,1,0:T(8,128)(2,1)} %bitcast.7, bf16[1,336,3072]{2,1,0:T(8,128)(2,1)} %bitcast.8, bf16[1,336,3072]{2,1,0:T(8,128)(2,1)} %wd_hbm.1), custom_call_target="tpu_custom_call" | custom-call | tf_op jit(solution)/shard_map/pallas_call | solution.py:400
  104.1 1.4 %copy.10 = bf16[128,192]{0,1:T(8,128)(2,1)} copy(bf16[128,192]{0,1:T(8,128)(2,1)} %bitcast.10) | data formatting | bytes 98304

commit v4 on v3

--- a/solution.py
+++ b/solution.py
@@ -17,9 +17,11 @@
 PAD = 80
 SRC = 4
 PART = 2 * CAP
-ROWS = 4 * PART
-NEAR, FAR, FAR_X, NEAR_X = 0, PART, 2 * PART, 3 * PART
-ROUND = (NEAR, FAR_X, FAR)
+HALF, ROWS = 2 * PART, 4 * PART
+GATHER = ((PART, PART), (HALF, PART), (0, PART))
+OVER_X = (HALF + PART, PART)
+SUMS = ((128, 160), (HALF, 128), (0, 128))
+SUMS_X = (HALF + 128, 160)
 MOST = ((4, 3), (3, 4), (3, 4))
 
 
@@ -35,15 +37,15 @@
 
 
 def kernel(
-    tok, ids, raw, wg_hbm, wu_hbm, wd_hbm, out, bal,
-    wg, wu, wd, wide, onehot, gates, slots, landing, gath, acc_g, acc_u, hid,
-    sums_s, sums_r, xs, xr, cross_s, cross_r, back_s, back_r, mix_s, mix_r, mass, bfly,
-    w_sem, tok_sem, y_send, y_recv, own_send, own_recv,
+    tok_hbm, ids_hbm, raw_hbm, wg_hbm, wu_hbm, wd_hbm, out, bal,
+    tok, ids, raw, wg, wu, wd, wide, onehot, gates, slots, landing, gath, acc_g, acc_u, hid,
+    sums_as, sums_ar, sums_bs, sums_br, xs, xr, cross_s, cross_r, back_s, back_r, mix_s, mix_r, mass, bfly,
+    in_sem, w_sem, tok_sem, y_send, y_recv, own_send, own_recv,
     g_send, g_recv, xf_send, xf_recv, r_send, r_recv, xs_send, xs_recv,
     cr_sem, bk_send, bk_recv, mx_sem, ms_send, ms_recv, bf_send, bf_recv,
 ):
     dp, ten, y = lax.axis_index("dp"), lax.axis_index("tensor"), lax.axis_index("expert")
-    feat, tokens = tok.shape
+    feat, tokens = tok_hbm.shape
     width = 2 * feat
     z, xl = ten // 2, lax.rem(ten, 2)
     turn = 1 - 2 * lax.rem(dp, 2)
@@ -68,18 +70,25 @@
     def flip(bit):
         return dp + bit - 2 * bit * lax.rem(dp // bit, 2)
 
+    small = [
+        pltpu.make_async_copy(src, dst, in_sem.at[i])
+        for i, (src, dst) in enumerate(((ids_hbm, ids), (raw_hbm, raw), (tok_hbm, tok)))
+    ]
+    for load in small:
+        load.start()
     loads = [
         pltpu.make_async_copy(src.at[0], dst, w_sem.at[i])
         for i, (src, dst) in enumerate(((wg_hbm, wg), (wu_hbm, wu), (wd_hbm, wd)))
     ]
-    for load in loads:
-        load.start()
-
     barrier = pltpu.get_barrier_semaphore()
     peers = [{"expert": lax.rem(y + i, NY)} for i in range(1, NY)]
     peers += [partner, ahead, behind] + [{"dp": flip(bit)} for bit in (1, 2, 4)]
     for peer in peers:
         pl.semaphore_signal(barrier, inc=1, device_id=peer, device_id_type=MESH)
+    for load in loads:
+        load.start()
+    for load in small:
+        load.wait()
 
     expert = lax.broadcasted_iota(jnp.int32, (16, tokens), 0)
     ids_v, raw_v = ids[...], raw[...]
@@ -141,7 +150,7 @@
         gath[pl.ds(z, 1), pl.ds(first, PART)] = jnp.concatenate(both, axis=0).astype(BF16)[None]
 
     def ring(part, way, hop, chunk):
-        rows = pl.ds(ROUND[part], PART)
+        rows = pl.ds(*GATHER[part])
         return remote(
             gath.at[chunk, rows], gath.at[chunk, rows],
             g_send.at[part, way, hop - 1], g_recv.at[part, way, hop - 1], (ahead, behind)[way],
@@ -149,21 +158,21 @@
 
     def over_x(chunk):
         return remote(
-            gath.at[chunk, pl.ds(NEAR, PART)], gath.at[chunk, pl.ds(NEAR_X, PART)],
+            gath.at[chunk, pl.ds(*GATHER[0])], gath.at[chunk, pl.ds(*OVER_X)],
             xf_send.at[chunk], xf_recv.at[chunk], partner,
         )
 
     own = remote(
-        gath.at[z, pl.ds(FAR, PART)], gath.at[z, pl.ds(FAR_X, PART)], own_send, own_recv, partner
+        gath.at[z, pl.ds(*GATHER[2])], gath.at[z, pl.ds(*GATHER[1])], own_send, own_recv, partner
     )
-    land(0, NEAR)
+    land(0, 0)
+    own.start()
+    ring(2, 0, 1, z).start()
+    ring(2, 1, 1, z).start()
+    land(2, PART)
     ring(0, 0, 1, z).start()
     ring(0, 1, 1, z).start()
     over_x(z).start()
-    land(2, FAR)
-    own.start()
-    ring(2, 0, 1, z).start()
-    ring(2, 1, 1, z).start()
 
     @pl.loop(0, NY - 1)
     def _(i):
@@ -206,29 +215,31 @@
                 if part == 0:
                     over_x(chunks[way]).start()
 
-        arrive(0, 0)
-        arrive(0, 1)
-
-        @pl.loop(0, jnp.where(hop == 1, 1, 2))
-        def _(i):
-            chunk = at((hop - 1) * (2 * i - 1))
+        def use_whole(chunk):
             over_x(chunk).wait_recv()
 
             @pl.loop(0, 2)
             def _(half):
                 use(chunk, pl.multiple_of(half * 2 * PART, 2 * PART), 2 * PART)
 
-        for part in (2, 1):
-            arrive(part, 0)
-            arrive(part, 1)
+        arrive(2, 0)
+        pl.when(hop < 4)(functools.partial(arrive, 2, 1))
+        arrive(0, 0)
+        arrive(0, 1)
+        use_whole(at(1 - hop))
+        arrive(1, 0)
+        pl.when(hop < 4)(functools.partial(arrive, 1, 1))
+        pl.when(hop > 1)(lambda: use_whole(at(hop - 1)))
 
     last = at(4)
-    use(last, FAR, 2 * PART)
-    activate(FAR, 2 * PART)
-
-    def product(first, dest):
+    for part in (2, 1):
+        ring(part, 1, 4, last).wait_recv()
+        use(last, *GATHER[part])
+        activate(*GATHER[part])
+
+    def product(rows, dest):
         cols = pl.ds(pl.multiple_of(dest * width, width), width)
-        return jnp.dot(hid[pl.ds(first, PART)], wd[:, cols], preferred_element_type=F32)
+        return jnp.dot(hid[pl.ds(*rows)], wd[:, cols], preferred_element_type=F32)
 
     def x_sum(dest):
         return remote(xs.at[dest], xr.at[dest], xs_send.at[dest], xs_recv.at[dest], partner)
@@ -236,36 +247,40 @@
     def give_x(i):
         away = (8 - i) // 2
         dest = at(away * (1 - 2 * lax.rem(i, 2)))
-        xs[pl.ds(dest, 1)] = product(NEAR_X, dest).astype(BF16)[None]
+        xs[pl.ds(dest, 1)] = product(SUMS_X, dest).astype(BF16)[None]
         x_sum(dest).start()
 
+    def boxes(part):
+        return (sums_as, sums_ar) if part == 0 else (sums_bs.at[part - 1], sums_br.at[part - 1])
+
     def sums(part, way, hop):
+        out_buf, in_buf = boxes(part)
         slot = way * 4 + hop - 1
         return remote(
-            sums_s.at[part, slot], sums_r.at[part, slot],
+            out_buf.at[slot], in_buf.at[slot],
             r_send.at[part, way, hop - 1], r_recv.at[part, way, hop - 1], (ahead, behind)[way],
         )
 
     def pass_on(part, way, hop, first=False):
         dest = at((MOST[part][way] + 1 - hop) * (1 - 2 * way))
-        value = product(ROUND[part], dest)
+        value = product(SUMS[part], dest)
         if part == 0:
             x_sum(dest).wait_recv()
             value = value + xr[dest].astype(F32)
         slot = way * 4 + hop - 1
         if not first:
             sums(part, way, hop - 1).wait_recv()
-            value = value + sums_r[part, slot - 1].astype(F32)
-        sums_s[part, pl.ds(slot, 1)] = value.astype(BF16)[None]
+            value = value + boxes(part)[1][slot - 1].astype(F32)
+        boxes(part)[0][pl.ds(slot, 1)] = value.astype(BF16)[None]
         sums(part, way, hop).start()
 
     for part in (1, 2):
         for way in (1, 0):
             pass_on(part, way, 1, True)
     over_x(last).wait_recv()
-    for first in (NEAR_X, NEAR):
-        use(last, first, PART)
-        activate(first, PART)
+    for rows in (OVER_X, GATHER[0]):
+        use(last, *rows)
+        activate(*rows)
 
     @pl.loop(0, 8)
     def _(i):
@@ -305,11 +320,11 @@
                 pair_copy(i).start()
 
     def total_of(part):
-        value = product(ROUND[part], z)
+        value = product(SUMS[part], z)
         for way in range(2):
             most = MOST[part][way]
             sums(part, way, most).wait_recv()
-            value = value + sums_r[part, way * 4 + most - 1].astype(F32)
+            value = value + boxes(part)[1][way * 4 + most - 1].astype(F32)
         return value
 
     cross_s[...] = total_of(1).astype(BF16)
@@ -329,18 +344,19 @@
             unless_own(j + i, to_source(j + i).start)
 
     x_sum(z).wait_recv()
-    give_back(total_of(0) + xr[z].astype(F32), 0)
+    after = total_of(0) + xr[z].astype(F32)
+    give_back(after[PART - 128 :], 2)
+    before = total_of(2)
+    crossing.wait_recv()
+    before = before + cross_r[...].astype(F32)
+    give_back(jnp.concatenate([before, after[: PART - 128]], axis=0), 0)
 
     @pl.when(xl == 0)
     def _():
         back_r[0] = back_s[0]
 
-    far = total_of(2)
-    crossing.wait_recv()
-    give_back(far + cross_r[...].astype(F32), 2)
-
     mixed = jnp.zeros((width, tokens), F32)
-    for j in range(SRC):
+    for j in (2, 3, 0, 1):
         unless_own(j, to_source(j).wait_recv)
         mixed = mixed + gates[j] * lax.dot_general(
             back_r[j], onehot[j], (((0,), (0,)), ((), ())), preferred_element_type=F32
@@ -403,9 +419,12 @@
             jax.ShapeDtypeStruct((feat, count), BF16),
             jax.ShapeDtypeStruct((1, 1), F32),
         ),
-        in_specs=[vmem, vmem, vmem, hbm, hbm, hbm],
+        in_specs=[hbm] * 6,
         out_specs=(vmem, vmem),
         scratch_shapes=[
+            pltpu.VMEM((feat, count), BF16),
+            pltpu.VMEM(turned[1].shape, jnp.int32),
+            pltpu.VMEM(turned[2].shape, F32),
             pltpu.VMEM((hidden, model), BF16),
             pltpu.VMEM((hidden, model), BF16),
             pltpu.VMEM((hidden, model), BF16),
@@ -418,18 +437,21 @@
             pltpu.VMEM((ROWS, hidden), F32),
             pltpu.VMEM((ROWS, hidden), F32),
             pltpu.VMEM((ROWS, hidden), BF16),
-            pltpu.VMEM((3, 8, PART, width), BF16),
-            pltpu.VMEM((3, 8, PART, width), BF16),
-            pltpu.VMEM((NZ, PART, width), BF16),
-            pltpu.VMEM((NZ, PART, width), BF16),
-            pltpu.VMEM((PART, width), BF16),
-            pltpu.VMEM((PART, width), BF16),
+            pltpu.VMEM((8, 160, width), BF16),
+            pltpu.VMEM((8, 160, width), BF16),
+            pltpu.VMEM((2, 8, 128, width), BF16),
+            pltpu.VMEM((2, 8, 128, width), BF16),
+            pltpu.VMEM((NZ, 160, width), BF16),
+            pltpu.VMEM((NZ, 160, width), BF16),
+            pltpu.VMEM((128, width), BF16),
+            pltpu.VMEM((128, width), BF16),
             pltpu.VMEM((SRC, PAD, width), BF16),
             pltpu.VMEM((SRC, PAD, width), BF16),
             pltpu.VMEM((feat, count), BF16),
             pltpu.VMEM((feat, count), BF16),
             pltpu.VMEM((NY, 8, 128), F32),
             pltpu.VMEM((6, 8, 128), F32),
+            dma((3,)),
             dma((3,)),
             dma((2,)),
             dma((SRC,)),

time: 108 us -> 106 us (0.981)
    pallas_call x1, Pallas kernels: 103 us -> 102 us  [body(): pl.pallas_call(kernel, out_shape=(jax.ShapeDtypeStruct((feat, count), BF1...]
where the time goes in v4:
time: 106 us; the launch traced here: 105 us
  Pallas kernels  102 us (96%)
  between operations  2.38 us (2%)
  local copies, waits for them, and re-layouts  1.42 us (1%)
    pallas_call x1, Pallas kernels, body(): pl.pallas_call(kernel, out_shape=(jax.ShapeDtypeStruct((feat, count), BF1...  102 us

profile of v4, /device:TPU:16, one launch (start us, length us, event | category | flops | bytes accessed | tf_op | source)
XLA Modules:
  0.0 105.3 jit_solution(18162352208347871178)
XLA Ops:
  0.6 101.5 %shard_map.77 = (bf16[192,128]{1,0:T(8,128)(2,1)}, f32[1,1]{1,0:T(1,128)}) custom-call(bf16[192,128]{1,0:T(8,128)(2,1)} %bitcast.9, s32[4,128]{1,0:T(4,128)} %bitcast.11, f32[4,128]{1,0:T(4,128)} %bitcast.12, bf16[1,336,3072]{2,1,0:T(8,128)(2,1)} %bitcast.7, bf16[1,336,3072]{2,1,0:T(8,128)(2,1)} %bitcast.8, bf16[1,336,3072]{2,1,0:T(8,128)(2,1)} %wd_hbm.1), custom_call_target="tpu_custom_call" | custom-call | tf_op jit(solution)/shard_map/pallas_call | solution.py:416
  102.2 1.4 %copy.10 = bf16[128,192]{0,1:T(8,128)(2,1)} copy(bf16[128,192]{0,1:T(8,128)(2,1)} %bitcast.10) | data formatting | bytes 98304

commit v5 on v4

--- a/solution.py
+++ b/solution.py
@@ -18,10 +18,8 @@
 SRC = 4
 PART = 2 * CAP
 HALF, ROWS = 2 * PART, 4 * PART
-GATHER = ((PART, PART), (HALF, PART), (0, PART))
-OVER_X = (HALF + PART, PART)
-SUMS = ((128, 160), (HALF, 128), (0, 128))
-SUMS_X = (HALF + 128, 160)
+PARTS = ((128, 160), (HALF, 128), (0, 128))
+OVER_X = (HALF + 128, 160)
 MOST = ((4, 3), (3, 4), (3, 4))
 
 
@@ -74,21 +72,25 @@
         pltpu.make_async_copy(src, dst, in_sem.at[i])
         for i, (src, dst) in enumerate(((ids_hbm, ids), (raw_hbm, raw), (tok_hbm, tok)))
     ]
-    for load in small:
-        load.start()
-    loads = [
-        pltpu.make_async_copy(src.at[0], dst, w_sem.at[i])
-        for i, (src, dst) in enumerate(((wg_hbm, wg), (wu_hbm, wu), (wd_hbm, wd)))
-    ]
+    for copy in small:
+        copy.start()
+    span = wg.shape[1] // 4
+
+    def load(i, quarter):
+        src, dst = ((wg_hbm, wg), (wu_hbm, wu), (wd_hbm, wd))[i]
+        cols = pl.ds(quarter * span, span)
+        return pltpu.make_async_copy(src.at[0, :, cols], dst.at[:, cols], w_sem.at[i, quarter])
+
     barrier = pltpu.get_barrier_semaphore()
     peers = [{"expert": lax.rem(y + i, NY)} for i in range(1, NY)]
     peers += [partner, ahead, behind] + [{"dp": flip(bit)} for bit in (1, 2, 4)]
     for peer in peers:
         pl.semaphore_signal(barrier, inc=1, device_id=peer, device_id_type=MESH)
-    for load in loads:
-        load.start()
-    for load in small:
-        load.wait()
+    for i in range(3):
+        for quarter in range(4):
+            load(i, quarter).start()
+    for copy in small:
+        copy.wait()
 
     expert = lax.broadcasted_iota(jnp.int32, (16, tokens), 0)
     ids_v, raw_v = ids[...], raw[...]
@@ -150,7 +152,7 @@
         gath[pl.ds(z, 1), pl.ds(first, PART)] = jnp.concatenate(both, axis=0).astype(BF16)[None]
 
     def ring(part, way, hop, chunk):
-        rows = pl.ds(*GATHER[part])
+        rows = pl.ds(*PARTS[part])
         return remote(
             gath.at[chunk, rows], gath.at[chunk, rows],
             g_send.at[part, way, hop - 1], g_recv.at[part, way, hop - 1], (ahead, behind)[way],
@@ -158,12 +160,12 @@
 
     def over_x(chunk):
         return remote(
-            gath.at[chunk, pl.ds(*GATHER[0])], gath.at[chunk, pl.ds(*OVER_X)],
+            gath.at[chunk, pl.ds(*PARTS[0])], gath.at[chunk, pl.ds(*OVER_X)],
             xf_send.at[chunk], xf_recv.at[chunk], partner,
         )
 
     own = remote(
-        gath.at[z, pl.ds(*GATHER[2])], gath.at[z, pl.ds(*GATHER[1])], own_send, own_recv, partner
+        gath.at[z, pl.ds(*PARTS[2])], gath.at[z, pl.ds(*PARTS[1])], own_send, own_recv, partner
     )
     land(0, 0)
     own.start()
@@ -183,8 +185,6 @@
     own.wait_recv()
     ring(1, 0, 1, z).start()
     ring(1, 1, 1, z).start()
-    for load in loads:
-        load.wait()
 
     def use(chunk, first, count):
         rows = pl.ds(first, count)
@@ -226,16 +226,25 @@
         pl.when(hop < 4)(functools.partial(arrive, 2, 1))
         arrive(0, 0)
         arrive(0, 1)
+
+        @pl.when(hop == 1)
+        def _():
+            for quarter in range(4):
+                load(0, quarter).wait()
+                load(1, quarter).wait()
+
         use_whole(at(1 - hop))
         arrive(1, 0)
         pl.when(hop < 4)(functools.partial(arrive, 1, 1))
         pl.when(hop > 1)(lambda: use_whole(at(hop - 1)))
 
+    for quarter in range(4):
+        load(2, quarter).wait()
     last = at(4)
     for part in (2, 1):
         ring(part, 1, 4, last).wait_recv()
-        use(last, *GATHER[part])
-        activate(*GATHER[part])
+        use(last, *PARTS[part])
+        activate(*PARTS[part])
 
     def product(rows, dest):
         cols = pl.ds(pl.multiple_of(dest * width, width), width)
@@ -247,7 +256,7 @@
     def give_x(i):
         away = (8 - i) // 2
         dest = at(away * (1 - 2 * lax.rem(i, 2)))
-        xs[pl.ds(dest, 1)] = product(SUMS_X, dest).astype(BF16)[None]
+        xs[pl.ds(dest, 1)] = product(OVER_X, dest).astype(BF16)[None]
         x_sum(dest).start()
 
     def boxes(part):
@@ -263,7 +272,7 @@
 
     def pass_on(part, way, hop, first=False):
         dest = at((MOST[part][way] + 1 - hop) * (1 - 2 * way))
-        value = product(SUMS[part], dest)
+        value = product(PARTS[part], dest)
         if part == 0:
             x_sum(dest).wait_recv()
             value = value + xr[dest].astype(F32)
@@ -278,7 +287,7 @@
         for way in (1, 0):
             pass_on(part, way, 1, True)
     over_x(last).wait_recv()
-    for rows in (OVER_X, GATHER[0]):
+    for rows in (OVER_X, PARTS[0]):
         use(last, *rows)
         activate(*rows)
 
@@ -319,8 +328,36 @@
                 bfly[2 * i] = bfly[2 * i - 2] + bfly[2 * i - 1]
                 pair_copy(i).start()
 
+    swap.wait_send()
+    own.wait_send()
+    for j in range(SRC):
+        unless_own(j, to_expert(j).wait_send)
+
+    @pl.loop(0, NY - 1)
+    def _(i):
+        mass_copy(i, y).wait_send()
+
+    @pl.loop(0, NZ)
+    def _(i):
+        over_x(i).wait_send()
+        x_sum(i).wait_send()
+
+    for i in range(2):
+        pair_copy(i).wait_send()
+
+    @pl.loop(1, 4)
+    def _(hop):
+        for part in range(3):
+            for way in range(2):
+                ring(part, way, hop, z).wait_send()
+                sums(part, way, hop).wait_send()
+
+    ring(0, 0, 4, z).wait_send()
+    ring(1, 1, 4, z).wait_send()
+    ring(2, 1, 4, z).wait_send()
+
     def total_of(part):
-        value = product(SUMS[part], z)
+        value = product(PARTS[part], z)
         for way in range(2):
             most = MOST[part][way]
             sums(part, way, most).wait_recv()
@@ -370,35 +407,13 @@
     every = (bfly[4] + bfly[5]) * (1.0 / (tokens * 64))
     bal[...] = NY * jnp.sum(every * every, axis=0, keepdims=True)[:, :1]
 
-    swap.wait_send()
-    own.wait_send()
     crossing.wait_send()
+    pair_copy(2).wait_send()
+    sums(0, 0, 4).wait_send()
+    sums(1, 1, 4).wait_send()
+    sums(2, 1, 4).wait_send()
     for j in range(SRC):
-        unless_own(j, to_expert(j).wait_send)
         unless_own(j, to_source(j).wait_send)
-
-    @pl.loop(0, NY - 1)
-    def _(i):
-        mass_copy(i, y).wait_send()
-
-    @pl.loop(0, NZ)
-    def _(i):
-        over_x(i).wait_send()
-        x_sum(i).wait_send()
-
-    for i in range(3):
-        pair_copy(i).wait_send()
-
-    @pl.loop(1, 5)
-    def _(hop):
-        for part in range(3):
-            for way in range(2):
-
-                def sent(part=part, way=way):
-                    ring(part, way, hop, z).wait_send()
-                    sums(part, way, hop).wait_send()
-
-                pl.when(hop <= MOST[part][way])(sent)
 
     mixing.wait_recv()
     out[...] = (jnp.where(xl == 0, left, right) + mix_r[...].astype(F32)).astype(BF16)
@@ -452,7 +467,7 @@
             pltpu.VMEM((NY, 8, 128), F32),
             pltpu.VMEM((6, 8, 128), F32),
             dma((3,)),
-            dma((3,)),
+            dma((3, 4)),
             dma((2,)),
             dma((SRC,)),
             dma((SRC,)),

time: 106 us -> 106 us (level)
  no operation moved by 1% of the time
where the time goes in v5:
time: 106 us
  Pallas kernels  102 us (96%)
  between operations  2.38 us (2%)
  local copies, waits for them, and re-layouts  1.42 us (1%)
    pallas_call x1, Pallas kernels, body(): pl.pallas_call(kernel, out_shape=(jax.ShapeDtypeStruct((feat, count), BF1...  102 us

profile of v5, /device:TPU:16, one launch (start us, length us, event | category | flops | bytes accessed | tf_op | source)
XLA Modules:
  0.0 105.9 jit_solution(5130754031171224273)
XLA Ops:
  0.6 102.1 %shard_map.77 = (bf16[192,128]{1,0:T(8,128)(2,1)}, f32[1,1]{1,0:T(1,128)}) custom-call(bf16[192,128]{1,0:T(8,128)(2,1)} %bitcast.9, s32[4,128]{1,0:T(4,128)} %bitcast.11, f32[4,128]{1,0:T(4,128)} %bitcast.12, bf16[1,336,3072]{2,1,0:T(8,128)(2,1)} %bitcast.7, bf16[1,336,3072]{2,1,0:T(8,128)(2,1)} %bitcast.8, bf16[1,336,3072]{2,1,0:T(8,128)(2,1)} %wd_hbm.1), custom_call_target="tpu_custom_call" | custom-call | tf_op jit(solution)/shard_map/pallas_call | solution.py:431
  102.8 1.4 %copy.10 = bf16[128,192]{0,1:T(8,128)(2,1)} copy(bf16[128,192]{0,1:T(8,128)(2,1)} %bitcast.10) | data formatting | bytes 98304

commit v6 on v4

--- a/solution.py
+++ b/solution.py
@@ -37,15 +37,15 @@
 
 
 def kernel(
-    tok_hbm, ids_hbm, raw_hbm, wg_hbm, wu_hbm, wd_hbm, out, bal,
-    tok, ids, raw, wg, wu, wd, wide, onehot, gates, slots, landing, gath, acc_g, acc_u, hid,
+    tok, ids, raw, wg_hbm, wu_hbm, wd_hbm, out, bal,
+    wg, wu, wd, wide, onehot, gates, slots, landing, gath, acc_g, acc_u, hid,
     sums_as, sums_ar, sums_bs, sums_br, xs, xr, cross_s, cross_r, back_s, back_r, mix_s, mix_r, mass, bfly,
-    in_sem, w_sem, tok_sem, y_send, y_recv, own_send, own_recv,
+    w_sem, tok_sem, y_send, y_recv, own_send, own_recv,
     g_send, g_recv, xf_send, xf_recv, r_send, r_recv, xs_send, xs_recv,
     cr_sem, bk_send, bk_recv, mx_sem, ms_send, ms_recv, bf_send, bf_recv,
 ):
     dp, ten, y = lax.axis_index("dp"), lax.axis_index("tensor"), lax.axis_index("expert")
-    feat, tokens = tok_hbm.shape
+    feat, tokens = tok.shape
     width = 2 * feat
     z, xl = ten // 2, lax.rem(ten, 2)
     turn = 1 - 2 * lax.rem(dp, 2)
@@ -70,25 +70,18 @@
     def flip(bit):
         return dp + bit - 2 * bit * lax.rem(dp // bit, 2)
 
-    small = [
-        pltpu.make_async_copy(src, dst, in_sem.at[i])
-        for i, (src, dst) in enumerate(((ids_hbm, ids), (raw_hbm, raw), (tok_hbm, tok)))
-    ]
-    for load in small:
-        load.start()
     loads = [
         pltpu.make_async_copy(src.at[0], dst, w_sem.at[i])
         for i, (src, dst) in enumerate(((wg_hbm, wg), (wu_hbm, wu), (wd_hbm, wd)))
     ]
+    for load in loads:
+        load.start()
+
     barrier = pltpu.get_barrier_semaphore()
     peers = [{"expert": lax.rem(y + i, NY)} for i in range(1, NY)]
     peers += [partner, ahead, behind] + [{"dp": flip(bit)} for bit in (1, 2, 4)]
     for peer in peers:
         pl.semaphore_signal(barrier, inc=1, device_id=peer, device_id_type=MESH)
-    for load in loads:
-        load.start()
-    for load in small:
-        load.wait()
 
     expert = lax.broadcasted_iota(jnp.int32, (16, tokens), 0)
     ids_v, raw_v = ids[...], raw[...]
@@ -419,12 +412,9 @@
             jax.ShapeDtypeStruct((feat, count), BF16),
             jax.ShapeDtypeStruct((1, 1), F32),
         ),
-        in_specs=[hbm] * 6,
+        in_specs=[vmem, vmem, vmem, hbm, hbm, hbm],
         out_specs=(vmem, vmem),
         scratch_shapes=[
-            pltpu.VMEM((feat, count), BF16),
-            pltpu.VMEM(turned[1].shape, jnp.int32),
-            pltpu.VMEM(turned[2].shape, F32),
             pltpu.VMEM((hidden, model), BF16),
             pltpu.VMEM((hidden, model), BF16),
             pltpu.VMEM((hidden, model), BF16),
@@ -452,7 +442,6 @@
             pltpu.VMEM((NY, 8, 128), F32),
             pltpu.VMEM((6, 8, 128), F32),
             dma((3,)),
-            dma((3,)),
             dma((2,)),
             dma((SRC,)),
             dma((SRC,)),
@@ -476,7 +465,7 @@
             dma((3,)),
         ],
         compiler_params=pltpu.CompilerParams(
-            collective_id=0, has_side_effects=True, vmem_limit_bytes=60 * 1024 * 1024
+            collective_id=0, has_side_effects=True, vmem_limit_bytes=52 * 1024 * 1024
         ),
     )(*turned, w_down)
     return (mixed.T, balance.reshape(()))

time: 106 us -> 107 us (level)
  local copies, waits for them, and re-layouts: 1.42 us -> 2.78 us
    unnamed x1 -> x7, local copies, waits for them, and re-layouts: 1.42 us -> 2.78 us
where the time goes in v6:
time: 107 us
  Pallas kernels  101 us (94%)
  local copies, waits for them, and re-layouts  2.78 us (3%)
  between operations  2.39 us (2%)
    pallas_call x1, Pallas kernels, body(): pl.pallas_call(kernel, out_shape=(jax.ShapeDtypeStruct((feat, count), BF1...  101 us
    unnamed x7, local copies, waits for them, and re-layouts  2.78 us

profile of v6, /device:TPU:16, one launch (start us, length us, event | category | flops | bytes accessed | tf_op | source)
XLA Modules:
  0.0 106.6 jit_solution(8871687600439006080)
XLA Ops:
  0.6 0.0 copy-start
  0.6 0.8 copy-done
  1.4 0.0 copy-start.1
  1.4 0.7 copy-done.1
  2.1 0.0 copy-start.2
  2.1 0.7 copy-done.2
  2.8 101.4 %shard_map.77 = (bf16[192,128]{1,0:T(8,128)(2,1)S(1)}, f32[1,1]{1,0:T(1,128)}) custom-call(bf16[192,128]{1,0:T(8,128)(2,1)S(1)} %bitcast.7, s32[4,128]{1,0:T(4,128)S(1)} %bitcast.9, f32[4,128]{1,0:T(4,128)S(1)} %bitcast.10, bf16[1,336,3072]{2,1,0:T(8,128)(2,1)} %bitcast.11, bf16[1,336,3072]{2,1,0:T(8,128)(2,1)} %bitcast.12, bf16[1,336,3072]{2,1,0:T(8,128)(2,1)} %wd_hbm.1), custom_call_target="tpu_custom_call" | custom-call | tf_op jit(solution)/shard_map/pallas_call | solution.py:409
  104.2 0.6 copy.10
Async XLA Ops:
  0.6 0.8 copy-start
  1.4 0.7 copy-start.1
  2.1 0.7 copy-start.2
